TPU v7x, 256 devices: a whole 4x4x8 slice. The times are simulated.
256 devices in a mesh: path: 16 (over z, core), col: 16 (over y, x).
Axes of the slice: x: 4, y: 4, z: 8, core: 2. Of those that a mesh axis runs over, the one named last changes fastest.
Arguments:
- exposure: bfloat16 [65536, 16384], P('path', 'col'), may hold values from -127 to 127
- scales: float32 [128, 65536], P('col', 'path'), may hold values from 0.003 to 0.27, as said below
- sketch: bfloat16 [32, 16384], P(None, 'col'), may hold values from -0.046875 to 0.046875
Outputs:
- basis: float32 [32, 65536], P(None, 'path')
- projected: float32 [32, 16384], P(None, 'col')
Inputs may be any that keep to these rules, and one draw needn't show every extreme that they name: `scales`: positive.
All inputs are finite; a program needn't handle non-finite values.
Results may differ from a plain program's by a relative error of at most 0.0003.
Values sent between devices are 32-bit elements; how exact they have to be, the bound alone decides.
No kernel may reach another device: no remote copies, remote signals or barrier semaphores. Data moves between devices by JAX's collectives and lax.ppermute only.
A program may use at most 64 MiB of HBM per device.

v0:
```python
import jax
import jax.numpy as jnp
from jax import lax
from jax.sharding import PartitionSpec as P

HIGH = lax.Precision.HIGHEST


def per_device(exposure, scales, sketch):
    row_count = exposure.shape[0]
    block_count = scales.shape[0]
    codes = exposure.reshape(row_count, block_count, 128)
    sketch3 = sketch.reshape(sketch.shape[0], block_count, 128)
    parts = lax.dot_general(
        sketch3, codes, (((2,), (2,)), ((1,), (1,))), preferred_element_type=jnp.float32
    )
    partial_value = jnp.sum(parts * scales[:, None, :], axis=0)
    sketched = lax.psum(partial_value, "col")
    gram_total = lax.psum(jnp.dot(sketched, sketched.T, precision=HIGH), "path")
    factor = jnp.linalg.cholesky(gram_total)
    orthonormal = lax.linalg.triangular_solve(factor, sketched, left_side=True, lower=True)
    weighted = orthonormal[None, :, :] * scales[:, None, :]
    term = lax.dot_general(
        weighted, codes.astype(jnp.float32), (((2,), (0,)), ((0,), (1,))), precision=HIGH
    )
    local_proj = term.transpose(1, 0, 2).reshape(orthonormal.shape[0], block_count * 128)
    projected = lax.psum(local_proj, "path")
    total_paths = row_count * lax.axis_size("path")
    basis = orthonormal * jnp.sqrt(jnp.float32(total_paths))
    return (basis, projected)


def solution(mesh):
    placed = (P("path", "col"), P("col", "path"), P(None, "col"))
    return jax.shard_map(
        per_device,
        mesh=mesh,
        in_specs=placed,
        out_specs=(P(None, "path"), P(None, "col")),
        check_vma=False,
    )
```

profile of v0, /device:TPU:1, one launch (start us, length us, event | category | flops | bytes accessed | tf_op | source)
XLA Modules:
  0.0 293.7 jit_solution(8979144331565636396)
XLA Ops:
  7.2 0.0 copy-start
  7.2 0.0 copy-start.1
  7.2 0.0 all-reduce.3.cloned.1.call-start
  7.2 0.8 copy-done
  8.0 7.3 %fusion.12 = f32[32,4096]{1,0:T(8,128)} fusion(f32[8,4096]{1,0:T(8,128)} %param.4, bf16[4096,1024]{1,0:T(8,128)(2,1)} %param.3, bf16[32,1024]{1,0:T(8,128)(2,1)S(1)} %copy-done), kind=kOutput, calls=%fused_computation.10 | convolution fusion | flops 270401536 | bytes 9109504 | tf_op jit(solution)/shard_map/dot_general | solution.py:14
  15.3 0.0 all-reduce.3.cloned.1.call-update
  15.3 0.0 all-reduce.5.cloned.1.call-start
  15.3 97.9 %all-reduce.3.cloned.1.call-done = f32[32,4096]{1,0:T(8,128)} async-done(((f32[32,4096]{1,0:T(8,128)}), f32[32,4096]{1,0:T(8,128)}) %all-reduce.3.cloned.1.call-update) | async-done | bytes 524304 | tf_op jit(solution)/shard_map/psum | solution.py:18
  113.2 1.8 fusion.26
  115.0 45.4 %psum.22 = f32[32,32]{0,1:T(8,128)S(1)} all-reduce(f32[32,32]{0,1:T(8,128)S(1)} %fusion.26), channel_id=1, replica_groups=mesh['path'=16,'col'=16] {'path'}, use_global_device_ids=true, to_apply=%region_2.0 | all-reduce | flops 1024 | bytes 8192 | tf_op jit(solution)/shard_map/psum | solution.py:19
  160.4 0.1 copy.13
  160.5 2.9 cholesky.16
  163.5 0.6 compare_reduce_fusion
  164.1 0.7 fusion.22
  164.8 2.4 custom-call.6
  167.2 2.5 broadcast_multiply_fusion
  169.7 0.0 copy-done.1
  169.7 6.3 %fusion.15 = f32[8,4,8,128]{3,2,1,0:T(8,128)S(1)} fusion(f32[32,4096]{1,0:T(8,128)S(1)} %get-tuple-element.3, f32[8,4096]{1,0:T(8,128)S(1)} %copy-done.1, bf16[4096,1024]{1,0:T(8,128)(2,1)} %param.3), kind=kOutput, calls=%fused_computation.11 | convolution fusion | flops 1611661312 | bytes 9175040 | tf_op jit(solution)/shard_map/dot_general | solution.py:23
  176.0 0.7 copy.39
  176.7 0.0 all-reduce.5.cloned.1.call-update
  176.7 108.7 %all-reduce.5.cloned.1.call-done = f32[32,1024]{1,0:T(8,128)} async-done(((f32[32,1024]{1,0:T(8,128)}), f32[32,1024]{1,0:T(8,128)}) %all-reduce.5.cloned.1.call-update) | async-done | bytes 131088 | tf_op jit(solution)/shard_map/psum | solution.py:27
  285.3 1.6 copy.42
  (2 shorter events, 0.0 us)
Async XLA Ops:
  7.2 0.8 copy-start
  7.2 162.5 %copy-start.1 = (f32[8,4096]{1,0:T(8,128)S(1)}, f32[8,4096]{1,0:T(8,128)}, u32[]{:S(2)}) copy-start(f32[8,4096]{1,0:T(8,128)} %param.4) | copy-start | bytes 393220
  7.2 106.0 %all-reduce.3.cloned.1.call-start = ((), (), s32[]{:S(2)}) async-start(), calls=%async_computation | async-start | bytes 1048576 | tf_op jit(solution)/shard_map/psum | solution.py:18
  15.3 270.1 %all-reduce.5.cloned.1.call-start = ((), (), s32[]{:S(2)}) async-start(), calls=%async_computation.1 | async-start | bytes 262144 | tf_op jit(solution)/shard_map/psum | solution.py:27
Sparse Core Ops, SparseCore 0:
  15.4 97.7 all-reduce.2
  176.8 108.4 all-reduce.4
where the time goes:
time: 294 us
  waiting for transfers between devices  207 us (70%)
  blocking collectives  45.4 us (15%)
  matrix products  17.8 us (6%)
  between operations  14.1 us (5%)
  other arithmetic  6.69 us (2%)
  local copies, waits for them, and re-layouts  3.09 us (1%)
    psum x1, waiting for transfers between devices, per_device(): projected = lax.psum(local_proj, 'path')  109 us
    psum x1, waiting for transfers between devices, per_device(): sketched = lax.psum(partial_value, 'col')  97.9 us
    psum x1, blocking collectives, per_device(): gram_total = lax.psum(jnp.dot(sketched, sketched.T, precision=HIGH), 'path')  45.4 us
    dot_general x1, matrix products, per_device(): lax.dot_general(sketch3, codes, (((2,), (2,)), ((1,), (1,))), preferred_e...  7.25 us
    dot_general x1, matrix products, per_device(): lax.dot_general(weighted, codes.astype(jnp.float32), (((2,), (0,)), ((0,)...  6.3 us
  transfers between devices with their start and end apart: 2, of which 2 were waited for; matrix products, arithmetic and copies ran while one was open for 0% of the time, Pallas kernels for 0%

commit v1 on v0

--- a/solution.py
+++ b/solution.py
@@ -2,8 +2,13 @@
 import jax.numpy as jnp
 from jax import lax
 from jax.sharding import PartitionSpec as P
+from jax.lax import all_gather
 
 HIGH = lax.Precision.HIGHEST
+
+
+def _press_quarters(frame, link_axis):
+    return all_gather(frame, axis_name=link_axis).sum(axis=0)
 
 
 def per_device(exposure, scales, sketch):
@@ -24,7 +29,7 @@
         weighted, codes.astype(jnp.float32), (((2,), (0,)), ((0,), (1,))), precision=HIGH
     )
     local_proj = term.transpose(1, 0, 2).reshape(orthonormal.shape[0], block_count * 128)
-    projected = lax.psum(local_proj, "path")
+    projected = _press_quarters(local_proj, "path")
     total_paths = row_count * lax.axis_size("path")
     basis = orthonormal * jnp.sqrt(jnp.float32(total_paths))
     return (basis, projected)

time: 294 us -> 228 us (0.78)
  waiting for transfers between devices: 207 us -> 139 us
    psum x1 -> x0, waiting for transfers between devices: 109 us -> none  [per_device(): projected = lax.psum(local_proj, 'path')]
    all_gather x0 -> x1, waiting for transfers between devices: none -> 41.3 us  [_press_quarters(): return all_gather(frame, axis_name=link_axis).sum(axis=0)]
where the time goes in v1:
time: 228 us; the launch traced here: 227 us
  waiting for transfers between devices  139 us (61%)
  blocking collectives  45.4 us (20%)
  matrix products  17.8 us (8%)
  between operations  14.1 us (6%)
  other arithmetic  9.06 us (4%)
    psum x1, waiting for transfers between devices, per_device(): sketched = lax.psum(partial_value, 'col')  97.9 us
    psum x1, blocking collectives, per_device(): gram_total = lax.psum(jnp.dot(sketched, sketched.T, precision=HIGH), 'path')  45.4 us
    all_gather x1, waiting for transfers between devices, _press_quarters(): return all_gather(frame, axis_name=link_axis).sum(axis=0)  41.3 us
    dot_general x1, matrix products, per_device(): lax.dot_general(sketch3, codes, (((2,), (2,)), ((1,), (1,))), preferred_e...  7.25 us
    dot_general x1, matrix products, per_device(): lax.dot_general(weighted, codes.astype(jnp.float32), (((2,), (0,)), ((0,)...  6.3 us
  transfers between devices with their start and end apart: 2, of which 2 were waited for; matrix products, arithmetic and copies ran while one was open for 0% of the time, Pallas kernels for 0%

profile of v1, /device:TPU:1, one launch (start us, length us, event | category | flops | bytes accessed | tf_op | source)
XLA Modules:
  0.0 227.3 jit_solution(17306317051651105078)
XLA Ops:
  7.2 0.0 copy-start
  7.2 0.0 copy-start.1
  7.2 0.0 all-reduce.2.cloned.1.call-start
  7.2 0.8 copy-done
  8.0 7.3 %fusion.12 = f32[32,4096]{1,0:T(8,128)} fusion(f32[8,4096]{1,0:T(8,128)} %param.4, bf16[4096,1024]{1,0:T(8,128)(2,1)} %param.3, bf16[32,1024]{1,0:T(8,128)(2,1)S(1)} %copy-done), kind=kOutput, calls=%fused_computation.10 | convolution fusion | flops 270401536 | bytes 9109504 | tf_op jit(solution)/shard_map/dot_general | solution.py:19
  15.3 0.0 all-reduce.2.cloned.1.call-update
  15.3 0.0 all-gather.2.cloned.1.call-start
  15.3 97.9 %all-reduce.2.cloned.1.call-done = f32[32,4096]{1,0:T(8,128)} async-done(((f32[32,4096]{1,0:T(8,128)}), f32[32,4096]{1,0:T(8,128)}) %all-reduce.2.cloned.1.call-update) | async-done | bytes 524304 | tf_op jit(solution)/shard_map/psum | solution.py:23
  113.2 1.8 fusion.26
  115.0 45.4 %psum.15 = f32[32,32]{0,1:T(8,128)S(1)} all-reduce(f32[32,32]{0,1:T(8,128)S(1)} %fusion.26), channel_id=1, replica_groups=mesh['path'=16,'col'=16] {'path'}, use_global_device_ids=true, to_apply=%region_2.0 | all-reduce | flops 1024 | bytes 8192 | tf_op jit(solution)/shard_map/psum | solution.py:24
  160.4 0.1 copy.19
  160.5 2.9 %cholesky.16 = f32[32,32]{1,0:T(8,128)S(1)} custom-call(f32[32,32]{1,0:T(8,128)S(1)} %fusion.25), custom_call_target="Cholesky" | custom-call | tf_op jit(solution)/shard_map/jit(cholesky)/cholesky | solution.py:25
  163.5 0.6 compare_reduce_fusion
  164.1 0.7 fusion.22
  164.8 2.4 %custom-call.6 = f32[1,32,32]{1,2,0:T(8,128)S(1)} custom-call(f32[1,32,32]{2,1,0:T(8,128)S(1)} %fusion.22), custom_call_target="InvertDiagBlocksLowerTriangular" | custom-call | tf_op jit(solution)/shard_map/triangular_solve | solution.py:26
  167.2 2.5 %broadcast_multiply_fusion = (f32[32,4096]{1,0:T(8,128)}, f32[32,4096]{1,0:T(8,128)S(1)}) fusion(f32[32,4096]{1,0:T(8,128)} %all-reduce.2.cloned.1.call-done, f32[1,32,32]{1,2,0:T(8,128)S(1)} %custom-call.6), kind=kOutput, calls=%fused_computation.12 | convolution fusion | flops 50462720 | bytes 1576960 | tf_op jit(solution)/shard_map/triangular_solve | solution.py:26
  169.7 0.0 copy-done.1
  169.7 6.3 %fusion.15 = f32[32,8,128]{2,0,1:T(8,128)S(1)} fusion(f32[32,4096]{1,0:T(8,128)S(1)} %get-tuple-element.3, f32[8,4096]{1,0:T(8,128)S(1)} %copy-done.1, bf16[4096,1024]{1,0:T(8,128)(2,1)} %param.3), kind=kOutput, calls=%fused_computation.11 | convolution fusion | flops 1611661312 | bytes 9175040 | tf_op jit(solution)/shard_map/dot_general | solution.py:28
  176.0 0.1 copy.21
  176.1 0.7 all_gather_reshape.3
  176.8 0.0 all-gather.2.cloned.1.call-update
  176.8 41.3 %all-gather.2.cloned.1.call-done = f32[16,32,1024]{2,1,0:T(8,128)} async-done(((f32[1,32,1024]{2,1,0:T(8,128)}), f32[16,32,1024]{2,1,0:T(8,128)}) %all-gather.2.cloned.1.call-update) | async-done | bytes 2097168 | tf_op jit(solution)/shard_map/all_gather | solution.py:11
  218.1 2.4 %reduce_sum.19 = f32[32,1024]{1,0:T(8,128)} reduce(f32[16,32,1024]{2,1,0:T(8,128)} %all-gather.2.cloned.1.call-done, f32[]{:T(128)} %constant.39.clone.1), dimensions={0}, to_apply=%region_5.6 | reduce | flops 491520 | bytes 2228228 | tf_op jit(solution)/shard_map/reduce_sum | solution.py:11
  (2 shorter events, 0.0 us)
Async XLA Ops:
  7.2 0.8 copy-start
  7.2 162.5 %copy-start.1 = (f32[8,4096]{1,0:T(8,128)S(1)}, f32[8,4096]{1,0:T(8,128)}, u32[]{:S(2)}) copy-start(f32[8,4096]{1,0:T(8,128)} %param.4) | copy-start | bytes 393220
  7.2 106.0 %all-reduce.2.cloned.1.call-start = ((), (), s32[]{:S(2)}) async-start(), calls=%async_computation | async-start | bytes 1048576 | tf_op jit(solution)/shard_map/psum | solution.py:23
  15.3 202.8 %all-gather.2.cloned.1.call-start = ((), (), s32[]{:S(2)}) async-start(), calls=%async_computation.1 | async-start | bytes 2228224 | tf_op jit(solution)/shard_map/all_gather | solution.py:11
Sparse Core Ops, SparseCore 0:
  15.4 97.7 all-reduce.1
  176.9 41.1 all-gather.1
